TPU v7x, 32 devices: a whole 2x2x4 slice. The times are simulated.
32 devices in a mesh: occ: 2 (over y), virt: 4 (over z), aux: 4 (over x, core).
Axes of the slice: x: 2, y: 2, z: 4, core: 2. Of those that a mesh axis runs over, the one named last changes fastest.
Arguments:
- factors: bfloat16 [3072, 4, 1024], P('aux', 'occ', 'virt'), may hold values from -2 to 2
- occ_energy: float32 [4], replicated, may hold values from -2 to -0.3
- virt_energy: float32 [1024], replicated, may hold values from 0.2 to 3
Outputs:
- density: float32 [3072, 4, 1024], P('aux', 'occ', 'virt')
All inputs are finite; a program needn't handle non-finite values.
Results may differ from a plain program's by a relative error of at most 0.0016.
Values may be sent and summed in bfloat16 or wider, within the bound.
A program may use at most 128 MiB of HBM per device.

v0:
```python
import jax
import jax.numpy as jnp
from jax import lax
from jax.sharding import PartitionSpec as P


def from_behind(value, axis, steps):
    count = lax.axis_size(axis)
    pairs = [(source, (source + steps) % count) for source in range(count)]
    return lax.ppermute(value, axis, pairs)


def energy_gap(eo_i, eo_j, ev_a, ev_all):
    return (
        eo_i[:, None, None, None]
        + eo_j[None, None, :, None]
        - ev_a[None, :, None, None]
        - ev_all[None, None, None, :]
    )


def contribute(local, partner, eo_i, eo_j, ev_a, ev_all):
    ints = jnp.einsum("qia,qjb->iajb", local, partner, preferred_element_type=jnp.float32)
    share = lax.psum_scatter(ints, "aux", scatter_dimension=1, tiled=True)
    part_width = share.shape[1]
    ev_share = lax.dynamic_slice_in_dim(ev_a, lax.axis_index("aux") * part_width, part_width)
    piece = (share / energy_gap(eo_i, eo_j, ev_share, ev_all)).astype(jnp.bfloat16)
    amps = lax.all_gather(piece, "aux", axis=1, tiled=True)
    return jnp.einsum("iajb,qjb->qia", amps, partner, preferred_element_type=jnp.float32)


def on_device(factors, occ_energy, virt_energy):
    n_occ = lax.axis_size("occ")
    steps = min(3, n_occ)
    occ_width = factors.shape[1]
    virt_width = factors.shape[2]
    occ_index = lax.axis_index("occ")
    eo_i = lax.dynamic_slice_in_dim(occ_energy, occ_index * occ_width, occ_width)
    ev_a = lax.dynamic_slice_in_dim(virt_energy, lax.axis_index("virt") * virt_width, virt_width)
    density = jnp.zeros(factors.shape, jnp.float32)
    shard = factors
    partner = factors
    for step in range(steps):
        if step > 0:
            shard = from_behind(shard, "occ", 1)
        partner = lax.all_gather(shard, "virt", axis=2, tiled=True)
        source = jnp.mod(occ_index - step + n_occ, n_occ)
        eo_j = lax.dynamic_slice_in_dim(occ_energy, source * occ_width, occ_width)
        density = density + contribute(factors, partner, eo_i, eo_j, ev_a, virt_energy)
    return density


def solution(mesh):
    return jax.shard_map(
        on_device,
        mesh=mesh,
        in_specs=(P("aux", "occ", "virt"), P(), P()),
        out_specs=P("aux", "occ", "virt"),
        check_vma=False,
    )
```

profile of v0, /device:TPU:0, one launch (start us, length us, event | category | flops | bytes accessed | tf_op | source)
XLA Modules:
  0.0 294.0 jit_solution(15931278481032087304)
XLA Ops:
  6.5 2.2 copy.4
  8.8 3.0 %collective-permute-start = (bf16[768,2,256]{2,0,1:T(8,128)(2,1)}, bf16[768,2,256]{2,0,1:T(8,128)(2,1)S(1)}, u32[]{:S(2)}, u32[]{:S(2)}) collective-permute-start(bf16[768,2,256]{2,0,1:T(8,128)(2,1)} %copy.4), channel_id=1, source_target_pairs={{0,16},{16,0},{1,17},{17,1},{2,18},{18,2},{3,19},{19,3},{4,20},{20... | collective-permute-start | bytes 2359304 | tf_op jit(solution)/shard_map/ppermute | solution.py:10
  11.8 17.8 %collective-permute-done = bf16[768,2,256]{2,0,1:T(8,128)(2,1)S(1)} collective-permute-done((bf16[768,2,256]{2,0,1:T(8,128)(2,1)}, bf16[768,2,256]{2,0,1:T(8,128)(2,1)S(1)}, u32[]{:S(2)}, u32[]{:S(2)}) %collective-permute-start) | collective-permute-done | bytes 786464 | tf_op jit(solution)/shard_map/ppermute | solution.py:10
  29.6 0.9 copy-done.1
  30.5 0.6 copy.7
  31.1 43.9 %all-gather.5.cloned.1.call-done = bf16[768,2,1024]{2,0,1:T(8,128)(2,1)} async-done(((bf16[768,2,256]{2,0,1:T(8,128)(2,1)}), bf16[768,2,1024]{2,0,1:T(8,128)(2,1)}) %all-gather.5.cloned.1.call-update) | async-done | bytes 3145744 | tf_op jit(solution)/shard_map/all_gather | solution.py:46
  75.1 5.6 %fusion.6 = f32[2,256,2,1024]{3,1,2,0:T(8,128)} fusion(bf16[768,2,256,1]{0,2,3,1:T(8,128)(2,1)S(1)} %copy.7, bf16[768,2,1024]{2,0,1:T(8,128)(2,1)} %all-gather.5.cloned.1.call-done), kind=kOutput, calls=%fused_computation.6 | convolution fusion | flops 1610612736 | bytes 8126464 | tf_op jit(solution)/shard_map/qia,qjb->iajb/dot_general | solution.py:23
  80.7 0.0 reduce-scatter.5.cloned.1.call-start
  80.8 57.5 %all-gather.9.cloned.1.call-done = bf16[768,2,1024]{2,0,1:T(8,128)(2,1)} async-done(((bf16[768,2,256]{2,0,1:T(8,128)(2,1)}), bf16[768,2,1024]{2,0,1:T(8,128)(2,1)}) %all-gather.9.cloned.1.call-update) | async-done | bytes 3145744 | tf_op jit(solution)/shard_map/all_gather | solution.py:46
  138.3 5.7 %fusion.2 = f32[2,256,2,1024]{3,1,2,0:T(8,128)} fusion(bf16[768,2,256,1]{0,2,3,1:T(8,128)(2,1)S(1)} %copy.7, bf16[768,2,1024]{2,0,1:T(8,128)(2,1)} %all-gather.9.cloned.1.call-done), kind=kOutput, calls=%fused_computation.2 | convolution fusion | flops 1610612736 | bytes 8126464 | tf_op jit(solution)/shard_map/qia,qjb->iajb/dot_general | solution.py:23
  144.1 0.6 copy-done.3
  144.7 0.1 dynamic_slice.19
  144.7 0.1 fusion.11
  144.8 0.1 broadcast_add_fusion
  144.9 0.1 broadcast_subtract_fusion
  145.0 38.6 %reduce-scatter.3.cloned.1.call-done = f32[2,64,2,1024]{3,1,2,0:T(8,128)} async-done(((f32[2,256,2,1024]{3,1,2,0:T(8,128)}), f32[2,64,2,1024]{3,1,2,0:T(8,128)}) %reduce-scatter.3.cloned.1.call-update) | async-done | bytes 1048592 | tf_op jit(solution)/shard_map/reduce_scatter | solution.py:24
  183.5 47.1 %reduce-scatter.5.cloned.1.call-done = f32[2,64,2,1024]{3,1,2,0:T(8,128)} async-done(((f32[2,256,2,1024]{3,1,2,0:T(8,128)}), f32[2,64,2,1024]{3,1,2,0:T(8,128)}) %reduce-scatter.5.cloned.1.call-update) | async-done | bytes 1048592 | tf_op jit(solution)/shard_map/reduce_scatter | solution.py:24
  230.6 2.9 divide_convert_fusion
  233.5 0.5 all-gather.11.cloned.1.call-update
  234.1 22.2 %all-gather.7.cloned.1.call-done = bf16[2,256,2,1024]{3,1,2,0:T(8,128)(2,1)} async-done(((bf16[2,64,2,1024]{3,1,2,0:T(8,128)(2,1)}), bf16[2,256,2,1024]{3,1,2,0:T(8,128)(2,1)}) %all-gather.7.cloned.1.call-update) | async-done | bytes 2097168 | tf_op jit(solution)/shard_map/all_gather | solution.py:28
  256.3 4.6 %fusion.4 = f32[2,256,768,1]{2,1,3,0:T(8,128)} fusion(bf16[2,256,2,1024]{3,1,2,0:T(8,128)(2,1)} %all-gather.7.cloned.1.call-done, bf16[768,2,1024]{2,0,1:T(8,128)(2,1)S(1)} %copy-done.4), kind=kOutput, calls=%fused_computation.4 | convolution fusion | flops 1610612736 | bytes 6815744 | tf_op jit(solution)/shard_map/iajb,qjb->qia/dot_general | solution.py:29
  260.8 19.5 %all-gather.11.cloned.1.call-done = bf16[2,256,2,1024]{3,1,2,0:T(8,128)(2,1)} async-done(((bf16[2,64,2,1024]{3,1,2,0:T(8,128)(2,1)}), bf16[2,256,2,1024]{3,1,2,0:T(8,128)(2,1)}) %all-gather.11.cloned.1.call-update) | async-done | bytes 2097168 | tf_op jit(solution)/shard_map/all_gather | solution.py:28
  280.3 4.8 %fusion.8 = f32[768,2,256]{0,2,1:T(8,128)S(1)} fusion(f32[2,256,768,1]{2,1,3,0:T(8,128)} %fusion.4, bf16[2,256,2,1024]{3,1,2,0:T(8,128)(2,1)} %all-gather.11.cloned.1.call-done, bf16[768,2,1024]{2,0,1:T(8,128)(2,1)} %all-gather.9.cloned.1.call-done), kind=kOutput, calls=%fused_computation.9 | convolution fusion | flops 1611005952 | bytes 8388608 | tf_op jit(solution)/shard_map/iajb,qjb->qia/dot_general | solution.py:29
  285.1 2.1 copy.6
  (18 shorter events, 0.3 us)
Async XLA Ops:
  6.5 24.0 %copy-start = (bf16[768,2,256]{2,1,0:T(2,128)(2,1)S(1)}, bf16[768,2,256]{2,1,0:T(2,128)(2,1)}, u32[]{:S(2)}) copy-start(bf16[768,2,256]{2,1,0:T(2,128)(2,1)} %param.3) | copy-start | bytes 2359300
  6.5 68.5 %all-gather.5.cloned.1.call-start = ((), (), s32[]{:S(2)}) async-start(), calls=%async_computation.2 | async-start | bytes 3932160 | tf_op jit(solution)/shard_map/all_gather | solution.py:46
  8.8 129.5 %all-gather.9.cloned.1.call-start = ((), (), s32[]{:S(2)}) async-start(), calls=%async_computation.5 | async-start | bytes 3932160 | tf_op jit(solution)/shard_map/all_gather | solution.py:46
  8.8 20.8 %collective-permute-start = (bf16[768,2,256]{2,0,1:T(8,128)(2,1)}, bf16[768,2,256]{2,0,1:T(8,128)(2,1)S(1)}, u32[]{:S(2)}, u32[]{:S(2)}) collective-permute-start(bf16[768,2,256]{2,0,1:T(8,128)(2,1)} %copy.4), channel_id=1, source_target_pairs={{0,16},{16,0},{1,17},{17,1},{2,18},{18,2},{3,19},{19,3},{4,20},{20... | collective-permute-start | bytes 2359304 | tf_op jit(solution)/shard_map/ppermute | solution.py:10
  29.6 0.9 copy-start.1
  30.5 153.0 %reduce-scatter.3.cloned.1.call-start = ((), (), s32[]{:S(2)}) async-start(), calls=%async_computation.3 | async-start | bytes 5242880 | tf_op jit(solution)/shard_map/reduce_scatter | solution.py:24
  80.7 149.9 %reduce-scatter.5.cloned.1.call-start = ((), (), s32[]{:S(2)}) async-start(), calls=%async_computation.6 | async-start | bytes 5242880 | tf_op jit(solution)/shard_map/reduce_scatter | solution.py:24
  144.0 0.7 copy-start.3
  144.0 0.8 copy-start.2
  144.0 112.3 %copy-start.4 = (bf16[768,2,1024]{2,0,1:T(8,128)(2,1)S(1)}, bf16[768,2,1024]{2,0,1:T(8,128)(2,1)}, u32[]{:S(2)}) copy-start(bf16[768,2,1024]{2,0,1:T(8,128)(2,1)} %all-gather.5.cloned.1.call-done) | copy-start | bytes 9437188
  144.0 112.2 %all-gather.7.cloned.1.call-start = ((), (), s32[]{:S(2)}) async-start(), calls=%async_computation.4 | async-start | bytes 2621440 | tf_op jit(solution)/shard_map/all_gather | solution.py:28
  233.5 46.8 %all-gather.11.cloned.1.call-start = ((), (), s32[]{:S(2)}) async-start(), calls=%async_computation.7 | async-start | bytes 2621440 | tf_op jit(solution)/shard_map/all_gather | solution.py:28
Sparse Core Ops, SparseCore 0:
  8.9 66.1 all-gather.4
  76.6 61.5 all-gather.8
  140.8 42.6 reduce-scatter.2
  186.1 44.4 reduce-scatter.4
  233.6 22.6 all-gather.6
  257.7 22.5 all-gather.10
where the time goes:
time: 294 us
  waiting for transfers between devices  247 us (84%)
  matrix products  20.7 us (7%)
  between operations  13.5 us (5%)
  local copies, waits for them, and re-layouts  6.47 us (2%)
  starting transfers between devices  3.24 us (1%)
  other arithmetic  3.01 us (1%)
    all_gather x2, waiting for transfers between devices, on_device(): partner = lax.all_gather(shard, 'virt', axis=2, tiled=True)  101 us
    reduce_scatter x2, waiting for transfers between devices, contribute(): share = lax.psum_scatter(ints, 'aux', scatter_dimension=1, tiled=True)  85.6 us
    all_gather x2, waiting for transfers between devices, contribute(): amps = lax.all_gather(piece, 'aux', axis=1, tiled=True)  41.7 us
    ppermute x1, waiting for transfers between devices, from_behind(): return lax.ppermute(value, axis, pairs)  17.8 us
    dot_general x2, matrix products, contribute(): jnp.einsum('qia,qjb->iajb', local, partner, preferred_element_type=jnp.fl...  11.3 us
    dot_general x2, matrix products, contribute(): jnp.einsum('iajb,qjb->qia', amps, partner, preferred_element_type=jnp.flo...  9.36 us
  transfers between devices with their start and end apart: 7, of which 7 were waited for; matrix products, arithmetic and copies ran while one was open for 6% of the time, Pallas kernels for 0%

commit v1 on v0

v1 whole, which is shorter than its diff:
```python
import functools

import jax
import jax.numpy as jnp
from jax import lax
from jax.experimental import pallas as pl
from jax.experimental.pallas import tpu as pltpu
from jax.sharding import PartitionSpec as P

AXES = ("occ", "virt", "aux")
WINDOW = 3
F32, BF16 = jnp.float32, jnp.bfloat16


def nearest(k, v, n):
    left, right = v, n - 1 - v
    short = jnp.minimum(left, right)
    alternating = v - (k + 1) // 2 if k % 2 else v + k // 2
    beyond = jnp.where(left <= right, k, n - 1 - k)
    return jnp.where(k <= 2 * short, alternating, beyond)


def kernel(
    n_occ, n_virt, n_aux, steps,
    f_ref, er_ref, ec_ref, out_ref,
    held, partner, part, sums, amps, dens, dsend, drecv,
    z_send, z_recv, y_send, y_recv, d_send, d_recv, s_send, s_recv, a_send, a_recv,
):
    o, v, u = (lax.axis_index(name) for name in AXES)
    rounds = n_aux.bit_length() - 1
    naux, block = f_ref.shape
    has_left, has_right = v >= 1, v <= n_virt - 2

    def remote(src, dst, send, recv, **where):
        at = {"occ": o, "virt": v, "aux": u, **where}
        return pltpu.make_async_remote_copy(
            src_ref=src, dst_ref=dst, send_sem=send, recv_sem=recv,
            device_id=tuple(at[name] for name in AXES), device_id_type=pl.DeviceIdType.MESH,
        )

    def flip(r):
        bit = 1 << r
        return u + bit - 2 * bit * (u // bit % 2)

    barrier = pltpu.get_barrier_semaphore()

    def greet(**where):
        at = {"occ": o, "virt": v, "aux": u, **where}
        pl.semaphore_signal(
            barrier, inc=1, device_id=tuple(at[name] for name in AXES), device_id_type=pl.DeviceIdType.MESH
        )

    offsets = sorted({d % n_occ for s in range(1, steps) for d in (s, -s)})
    for d in offsets:
        greet(occ=lax.rem(o + d, n_occ))
    for r in range(rounds):
        greet(aux=flip(r))

    @pl.when(has_left)
    def _():
        greet(virt=v - 1)

    @pl.when(has_right)
    def _():
        greet(virt=v + 1)

    ends = jnp.minimum(v, 1) + jnp.minimum(n_virt - 1 - v, 1)
    pl.semaphore_wait(barrier, len(offsets) + rounds + ends)

    def along(src, w, to_right):
        if to_right:
            return remote(src, held.at[w], z_send.at[0, w], z_recv.at[w], virt=v + 1)
        return remote(src, held.at[w], z_send.at[1, w], z_recv.at[w], virt=v - 1)

    @pl.when(has_right)
    def _():
        along(f_ref, v, True).start()

    @pl.when(has_left)
    def _():
        along(f_ref, v, False).start()

    def across(s):
        return remote(
            f_ref, partner.at[s - 1], y_send.at[s - 1], y_recv.at[s - 1], occ=lax.rem(o - s + n_occ, n_occ)
        )

    for s in range(1, steps):
        across(s).start()

    held[pl.ds(v, 1)] = f_ref[...].reshape(1, naux, block)

    def arrive(k):
        @pl.when(v >= k)
        def _():
            w = v - k
            along(held.at[w], w, True).wait_recv()

            @pl.when(has_right)
            def _():
                along(held.at[w], w, True).start()

        @pl.when(v + k <= n_virt - 1)
        def _():
            w = v + k
            along(held.at[w], w, False).wait_recv()

            @pl.when(has_left)
            def _():
                along(held.at[w], w, False).start()

    def size(r):
        return block >> (r + 1)

    def bases(r):
        base = 0
        for t in range(r):
            base = base + (u // (1 << t) % 2) * size(t)
        bit = u // (1 << r) % 2
        keep = pl.multiple_of(base + bit * size(r), size(r))
        give = pl.multiple_of(base + (1 - bit) * size(r), size(r))
        return keep, give

    sum_at = [sum(size(t) for t in range(r)) for r in range(rounds)]

    def sum_copy(p, r):
        _, give = bases(r)
        return remote(
            part.at[p, pl.ds(give, size(r))], sums.at[p, pl.ds(sum_at[r], size(r))],
            s_send.at[p, r], s_recv.at[p, r], aux=flip(r),
        )

    def amp_copy(p, r):
        keep, _ = bases(r)
        rows = pl.ds(keep, size(r))
        return remote(amps.at[p, rows], amps.at[p, rows], a_send.at[p, r], a_recv.at[p, r], aux=flip(r))

    def left_block(k):
        return held[pl.ds(nearest(k, v, n_virt), 1)].reshape(naux, block)

    def integrals(p, k, s):
        cols = f_ref[...] if s == 0 else partner[s - 1]
        part[p] = lax.dot_general(left_block(k), cols, (((0,), (0,)), ((), ())), preferred_element_type=F32)
        sum_copy(p, 0).start()

    def add(p, r):
        keep, _ = bases(r)
        sum_copy(p, r).wait_recv()
        rows = pl.ds(keep, size(r))
        part[p, rows] = part[p, rows] + sums[p, pl.ds(sum_at[r], size(r))]
        if r + 1 < rounds:
            sum_copy(p, r + 1).start()

    def amplitudes(p, k, s):
        keep, _ = bases(rounds - 1)
        rows = pl.ds(keep, size(rounds - 1))
        gap = er_ref[pl.ds(nearest(k, v, n_virt), 1)].reshape(size(rounds - 1), 1) + ec_ref[s : s + 1]
        amps[p, rows] = (part[p, rows] / gap).astype(BF16)
        amp_copy(p, rounds - 1).start()

    def spread(p, r):
        amp_copy(p, r).wait_recv()
        if r > 0:
            amp_copy(p, r - 1).start()

    def contract(p, k, s):
        term = lax.dot_general(left_block(k), amps[p], (((1,), (0,)), ((), ())), preferred_element_type=F32)
        if k == 0:
            dens[s] = term
        else:
            dens[s] = dens[s] + term

    def back(s):
        return remote(
            dsend.at[s - 1], drecv.at[s - 1], d_send.at[s - 1], d_recv.at[s - 1], occ=lax.rem(o + s, n_occ)
        )

    groups = [[(0, 0)]]
    groups.append([(0, s) for s in range(1, steps)])
    for k in range(1, n_virt):
        pieces = [(k, s) for s in reversed(range(steps))]
        if k == 1:
            groups[1] += pieces
        else:
            groups.append(pieces)

    number = 0
    for g, group in enumerate(groups):
        if g > 0:
            arrive(g)
        if g == 1:
            for s in range(1, steps):
                across(s).wait_recv()
        named = []
        for k, s in group:
            named.append((number, k, s))
            number += 1
        for p, k, s in named:
            integrals(p, k, s)
        for r in range(rounds):
            for p, k, s in named:
                add(p, r)
                if r == rounds - 1:
                    amplitudes(p, k, s)
        for p, k, s in named:
            for r in reversed(range(rounds)):
                spread(p, r)
            contract(p, k, s)
            if k == n_virt - 1 and s > 0:
                dsend[s - 1] = dens[s].astype(BF16)
                back(s).start()

    out_ref[...] = dens[0]
    for s in range(1, steps):
        back(s).wait_recv()
        out_ref[...] += drecv[s - 1].astype(F32)

    for s in range(1, steps):
        back(s).wait_send()
        across(s).wait_send()
    for p in range(number):
        for r in range(rounds):
            sum_copy(p, r).wait_send()
            amp_copy(p, r).wait_send()
    for k in range(n_virt - 1):

        @pl.when((v >= k) & has_right)
        def _():
            along(held.at[v - k], v - k, True).wait_send()

        @pl.when((v + k <= n_virt - 1) & has_left)
        def _():
            along(held.at[v + k], v + k, False).wait_send()


def on_device(sizes, factors, occ_energy, virt_energy):
    n_occ, n_virt, n_aux = sizes
    steps = min(WINDOW, n_occ)
    naux, occ_width, virt_width = factors.shape
    block = occ_width * virt_width
    rounds = n_aux.bit_length() - 1
    rows = block // n_aux
    o, v, u = (lax.axis_index(name) for name in AXES)

    eo = occ_energy.reshape(n_occ, occ_width)
    ev = virt_energy.reshape(n_virt, virt_width)
    eo_own = lax.dynamic_index_in_dim(eo, o, 0, keepdims=False)
    er = (eo_own[None, :, None] - ev[:, None, :]).reshape(n_virt, block)
    first = 0
    for r in range(rounds):
        first = first + ((u >> r) & 1) * (block >> (r + 1))
    er = lax.dynamic_slice_in_dim(er, first, rows, 1).reshape(n_virt, rows, 1)
    ev_own = lax.dynamic_index_in_dim(ev, v, 0, keepdims=False)
    eo_cols = jnp.roll(eo, -o, 0)[:steps]
    ec = (eo_cols[:, :, None] - ev_own[None, None, :]).reshape(steps, block)

    pieces = n_virt * steps
    dma = pltpu.SemaphoreType.DMA
    flops = 4 * pieces * naux * block * block
    density = pl.pallas_call(
        functools.partial(kernel, n_occ, n_virt, n_aux, steps),
        out_shape=jax.ShapeDtypeStruct((naux, block), F32),
        in_specs=[pl.BlockSpec(memory_space=pltpu.VMEM)] * 3,
        out_specs=pl.BlockSpec(memory_space=pltpu.VMEM),
        scratch_shapes=[
            pltpu.VMEM((n_virt, naux, block), BF16),
            pltpu.VMEM((steps - 1, naux, block), BF16),
            pltpu.VMEM((pieces, block, block), F32),
            pltpu.VMEM((pieces, block - rows, block), F32),
            pltpu.VMEM((pieces, block, block), BF16),
            pltpu.VMEM((steps, naux, block), F32),
            pltpu.VMEM((steps - 1, naux, block), BF16),
            pltpu.VMEM((steps - 1, naux, block), BF16),
            dma((2, n_virt)), dma((n_virt,)),
            dma((steps - 1,)), dma((steps - 1,)),
            dma((steps - 1,)), dma((steps - 1,)),
            dma((pieces, rounds)), dma((pieces, rounds)),
            dma((pieces, rounds)), dma((pieces, rounds)),
        ],
        compiler_params=pltpu.CompilerParams(
            collective_id=0, has_side_effects=True, vmem_limit_bytes=60 << 20
        ),
        cost_estimate=pl.CostEstimate(flops=flops, bytes_accessed=6 * naux * block, transcendentals=0),
    )(factors.reshape(naux, block), er, ec)
    return density.reshape(factors.shape)


def solution(mesh):
    sizes = tuple(mesh.shape[name] for name in AXES)
    return jax.shard_map(
        functools.partial(on_device, sizes),
        mesh=mesh,
        in_specs=(P("aux", "occ", "virt"), P(), P()),
        out_specs=P("aux", "occ", "virt"),
        check_vma=False,
    )
```

time: 294 us -> 128 us (0.44)
  waiting for transfers between devices: 247 us -> 0 us
  Pallas kernels: 0 us -> 119 us
  matrix products: 20.7 us -> 0 us
  between operations: 13.5 us -> 0.03 us
  starting transfers between devices: 3.24 us -> 0 us
    all_gather x4 -> x0, waiting for transfers between devices: 143 us -> none  [the longest x2 101 us: on_device(): partner = lax.all_gather(shard, 'virt', axis=2, tiled=True)]
    pallas_call x0 -> x1, Pallas kernels: none -> 119 us  [on_device(): pl.pallas_call(functools.partial(kernel, n_occ, n_virt, n_aux, steps), ou...]
    reduce_scatter x2 -> x0, waiting for transfers between devices: 85.6 us -> none  [contribute(): share = lax.psum_scatter(ints, 'aux', scatter_dimension=1, tiled=True)]
    dot_general x4 -> x0, matrix products: 20.7 us -> none  [the longest x2 11.3 us: contribute(): jnp.einsum('qia,qjb->iajb', local, partner, preferred_element_type=jnp.fl...]
    ppermute x1 -> x0, waiting for transfers between devices: 17.8 us -> none  [from_behind(): return lax.ppermute(value, axis, pairs)]
    reshape x0 -> x3, local copies, waits for them, and re-layouts: none -> 4.64 us  [the longest x1 3.05 us: on_device(): return density.reshape(factors.shape)]
    ppermute x1 -> x0, starting transfers between devices: 3.03 us -> none  [from_behind(): return lax.ppermute(value, axis, pairs)]
  transfers between devices with their start and end apart: 7 -> 0, of which waited for: 7 -> 0; matrix products, arithmetic and copies ran while one was open for 6% -> 0% of each run, Pallas kernels for 0% -> 0%
where the time goes in v1:
time: 128 us; the launch traced here: 127 us
  Pallas kernels  119 us (93%)
  local copies, waits for them, and re-layouts  7.79 us (6%)
    pallas_call x1, Pallas kernels, on_device(): pl.pallas_call(functools.partial(kernel, n_occ, n_virt, n_aux, steps), ou...  119 us
    reshape x1, local copies, waits for them, and re-layouts, on_device(): return density.reshape(factors.shape)  3.05 us

profile of v1, /device:TPU:0, one launch (start us, length us, event | category | flops | bytes accessed | tf_op | source)
XLA Modules:
  0.0 127.1 jit_solution(16159992551518042899)
XLA Ops:
  0.0 0.7 reshape.26
  0.8 0.1 broadcast_bitcast_fusion.3
  0.8 0.1 dynamic-slice
  0.9 0.1 broadcast_bitcast_fusion.1
  1.0 0.7 sub.54
  1.7 0.6 broadcast_subtract_fusion.ec_ref
  2.3 0.9 copy.4.er_ref
  3.2 2.2 %copy.6 = bf16[96,8,2,256]{3,1,2,0:T(8,128)(2,1)} copy(bf16[96,8,2,256]{3,2,1,0:T(2,128)(2,1)} %bitcast.19) | data formatting | bytes 1572864
  5.4 118.7 %shard_map.37 = f32[768,512]{1,0:T(8,128)} custom-call(bf16[768,512]{1,0:T(8,128)(2,1)} %bitcast.20, f32[4,128,1]{2,1,0:T(8,128)} %copy.4.er_ref, f32[2,512]{1,0:T(2,128)} %broadcast_subtract_fusion.ec_ref), custom_call_target="tpu_custom_call" | custom-call | flops 6442450944 | bytes 2359296 | tf_op jit(solution)/shard_map/pallas_call | solution.py:260
  124.1 3.0 %reshape.28 = f32[768,2,256]{2,1,0:T(2,128)} reshape(f32[768,512]{1,0:T(8,128)} %shard_map.37) | data formatting | bytes 3145728 | tf_op jit(solution)/shard_map/reshape | solution.py:285
  (11 shorter events, 0.1 us)

commit v2 on v1

--- a/solution.py
+++ b/solution.py
@@ -9,6 +9,8 @@
 
 AXES = ("occ", "virt", "aux")
 WINDOW = 3
+HALVES = 2
+SPAN = 120.0
 F32, BF16 = jnp.float32, jnp.bfloat16
 
 
@@ -20,11 +22,22 @@
     return jnp.where(k <= 2 * short, alternating, beyond)
 
 
+def encode(x, top):
+    z = jnp.exp2(jnp.abs(x) * (2 * SPAN / top) - SPAN)
+    return jnp.where(x < 0, -z, z).astype(BF16)
+
+
+def decode(z, top):
+    z = z.astype(F32)
+    x = (jnp.log2(jnp.abs(z)) + SPAN) * (top * (0.5 / SPAN))
+    return jnp.where(z < 0, -x, x)
+
+
 def kernel(
     n_occ, n_virt, n_aux, steps,
     f_ref, er_ref, ec_ref, out_ref,
-    held, partner, part, sums, amps, dens, dsend, drecv,
-    z_send, z_recv, y_send, y_recv, d_send, d_recv, s_send, s_recv, a_send, a_recv,
+    held, partner, part, sums, code_out, code_in, top_out, top_in, amps, dens, dsend, drecv,
+    z_send, z_recv, y_send, y_recv, d_send, d_recv, s_send, s_recv, t_send, t_recv, a_send, a_recv,
 ):
     o, v, u = (lax.axis_index(name) for name in AXES)
     rounds = n_aux.bit_length() - 1
@@ -67,18 +80,23 @@
     ends = jnp.minimum(v, 1) + jnp.minimum(n_virt - 1 - v, 1)
     pl.semaphore_wait(barrier, len(offsets) + rounds + ends)
 
-    def along(src, w, to_right):
+    deep = naux // HALVES
+
+    def along(src, w, h, to_right):
+        rows = pl.ds(h * deep, deep)
         if to_right:
-            return remote(src, held.at[w], z_send.at[0, w], z_recv.at[w], virt=v + 1)
-        return remote(src, held.at[w], z_send.at[1, w], z_recv.at[w], virt=v - 1)
+            return remote(src.at[rows], held.at[w, rows], z_send.at[0, w, h], z_recv.at[w, h], virt=v + 1)
+        return remote(src.at[rows], held.at[w, rows], z_send.at[1, w, h], z_recv.at[w, h], virt=v - 1)
 
     @pl.when(has_right)
     def _():
-        along(f_ref, v, True).start()
+        for h in range(HALVES):
+            along(f_ref, v, h, True).start()
 
     @pl.when(has_left)
     def _():
-        along(f_ref, v, False).start()
+        for h in range(HALVES):
+            along(f_ref, v, h, False).start()
 
     def across(s):
         return remote(
@@ -90,24 +108,24 @@
 
     held[pl.ds(v, 1)] = f_ref[...].reshape(1, naux, block)
 
-    def arrive(k):
+    def arrive(k, h):
         @pl.when(v >= k)
         def _():
             w = v - k
-            along(held.at[w], w, True).wait_recv()
+            along(held.at[w], w, h, True).wait_recv()
 
             @pl.when(has_right)
             def _():
-                along(held.at[w], w, True).start()
+                along(held.at[w], w, h, True).start()
 
         @pl.when(v + k <= n_virt - 1)
         def _():
             w = v + k
-            along(held.at[w], w, False).wait_recv()
+            along(held.at[w], w, h, False).wait_recv()
 
             @pl.when(has_left)
             def _():
-                along(held.at[w], w, False).start()
+                along(held.at[w], w, h, False).start()
 
     def size(r):
         return block >> (r + 1)
@@ -121,14 +139,18 @@
         give = pl.multiple_of(base + (1 - bit) * size(r), size(r))
         return keep, give
 
-    sum_at = [sum(size(t) for t in range(r)) for r in range(rounds)]
+    code_at = [0] + [sum(size(t) for t in range(1, r)) for r in range(1, rounds)]
 
     def sum_copy(p, r):
-        _, give = bases(r)
-        return remote(
-            part.at[p, pl.ds(give, size(r))], sums.at[p, pl.ds(sum_at[r], size(r))],
-            s_send.at[p, r], s_recv.at[p, r], aux=flip(r),
-        )
+        if r == 0:
+            src, dst = part.at[p, pl.ds(bases(0)[1], size(0))], sums.at[p]
+        else:
+            rows = pl.ds(code_at[r], size(r))
+            src, dst = code_out.at[p, rows], code_in.at[p, rows]
+        return remote(src, dst, s_send.at[p, r], s_recv.at[p, r], aux=flip(r))
+
+    def top_copy(p, r):
+        return remote(top_out.at[p, r], top_in.at[p, r], t_send.at[p, r], t_recv.at[p, r], aux=flip(r))
 
     def amp_copy(p, r):
         keep, _ = bases(r)
@@ -147,8 +169,18 @@
         keep, _ = bases(r)
         sum_copy(p, r).wait_recv()
         rows = pl.ds(keep, size(r))
-        part[p, rows] = part[p, rows] + sums[p, pl.ds(sum_at[r], size(r))]
+        if r == 0:
+            part[p, rows] = part[p, rows] + sums[p]
+        else:
+            top_copy(p, r).wait_recv()
+            part[p, rows] = part[p, rows] + decode(code_in[p, pl.ds(code_at[r], size(r))], top_in[p, r, :1, :1])
         if r + 1 < rounds:
+            _, give = bases(r + 1)
+            x = part[p, pl.ds(give, size(r + 1))]
+            top = jnp.maximum(jnp.max(jnp.abs(x), axis=(0, 1), keepdims=True), 1e-30)
+            top_out[p, r + 1] = jnp.broadcast_to(top, top_out.shape[2:])
+            code_out[p, pl.ds(code_at[r + 1], size(r + 1))] = encode(x, top)
+            top_copy(p, r + 1).start()
             sum_copy(p, r + 1).start()
 
     def amplitudes(p, k, s):
@@ -184,10 +216,19 @@
         else:
             groups.append(pieces)
 
+    def finish(p, k, s):
+        for r in reversed(range(rounds)):
+            spread(p, r)
+        contract(p, k, s)
+        if k == n_virt - 1 and s > 0:
+            dsend[s - 1] = dens[s].astype(BF16)
+            back(s).start()
+
     number = 0
     for g, group in enumerate(groups):
         if g > 0:
-            arrive(g)
+            for h in range(HALVES):
+                arrive(g, h)
         if g == 1:
             for s in range(1, steps):
                 across(s).wait_recv()
@@ -197,18 +238,17 @@
             number += 1
         for p, k, s in named:
             integrals(p, k, s)
+        last = g == len(groups) - 1
         for r in range(rounds):
             for p, k, s in named:
                 add(p, r)
                 if r == rounds - 1:
                     amplitudes(p, k, s)
-        for p, k, s in named:
-            for r in reversed(range(rounds)):
-                spread(p, r)
-            contract(p, k, s)
-            if k == n_virt - 1 and s > 0:
-                dsend[s - 1] = dens[s].astype(BF16)
-                back(s).start()
+                    if last:
+                        finish(p, k, s)
+        if not last:
+            for p, k, s in named:
+                finish(p, k, s)
 
     out_ref[...] = dens[0]
     for s in range(1, steps):
@@ -221,16 +261,20 @@
     for p in range(number):
         for r in range(rounds):
             sum_copy(p, r).wait_send()
+            if r > 0:
+                top_copy(p, r).wait_send()
             amp_copy(p, r).wait_send()
     for k in range(n_virt - 1):
 
         @pl.when((v >= k) & has_right)
         def _():
-            along(held.at[v - k], v - k, True).wait_send()
+            for h in range(HALVES):
+                along(held.at[v - k], v - k, h, True).wait_send()
 
         @pl.when((v + k <= n_virt - 1) & has_left)
         def _():
-            along(held.at[v + k], v + k, False).wait_send()
+            for h in range(HALVES):
+                along(held.at[v + k], v + k, h, False).wait_send()
 
 
 def on_device(sizes, factors, occ_energy, virt_energy):
@@ -266,14 +310,19 @@
             pltpu.VMEM((n_virt, naux, block), BF16),
             pltpu.VMEM((steps - 1, naux, block), BF16),
             pltpu.VMEM((pieces, block, block), F32),
-            pltpu.VMEM((pieces, block - rows, block), F32),
+            pltpu.VMEM((pieces, block // 2, block), F32),
+            pltpu.VMEM((pieces, block // 2 - rows, block), BF16),
+            pltpu.VMEM((pieces, block // 2 - rows, block), BF16),
+            pltpu.VMEM((pieces, rounds, 8, 128), F32),
+            pltpu.VMEM((pieces, rounds, 8, 128), F32),
             pltpu.VMEM((pieces, block, block), BF16),
             pltpu.VMEM((steps, naux, block), F32),
             pltpu.VMEM((steps - 1, naux, block), BF16),
             pltpu.VMEM((steps - 1, naux, block), BF16),
-            dma((2, n_virt)), dma((n_virt,)),
+            dma((2, n_virt, HALVES)), dma((n_virt, HALVES)),
             dma((steps - 1,)), dma((steps - 1,)),
             dma((steps - 1,)), dma((steps - 1,)),
+            dma((pieces, rounds)), dma((pieces, rounds)),
             dma((pieces, rounds)), dma((pieces, rounds)),
             dma((pieces, rounds)), dma((pieces, rounds)),
         ],

time: 128 us -> 113 us (0.88)
  Pallas kernels: 119 us -> 104 us
    pallas_call x1, Pallas kernels: 119 us -> 104 us  [on_device(): pl.pallas_call(functools.partial(kernel, n_occ, n_virt, n_aux, steps), ou...]
where the time goes in v2:
time: 113 us
  Pallas kernels  104 us (92%)
  local copies, waits for them, and re-layouts  7.79 us (7%)
    pallas_call x1, Pallas kernels, on_device(): pl.pallas_call(functools.partial(kernel, n_occ, n_virt, n_aux, steps), ou...  104 us
    reshape x1, local copies, waits for them, and re-layouts, on_device(): return density.reshape(factors.shape)  3.05 us
    unnamed x9, local copies, waits for them, and re-layouts  2.35 us

profile of v2, /device:TPU:0, one launch (start us, length us, event | category | flops | bytes accessed | tf_op | source)
XLA Modules:
  0.0 112.8 jit_solution(2109680504605511741)
XLA Ops:
  0.0 0.7 reshape.26
  0.8 0.1 broadcast_bitcast_fusion.3
  0.8 0.1 dynamic-slice
  0.9 0.1 broadcast_bitcast_fusion.1
  1.0 0.7 sub.54
  1.7 0.6 broadcast_subtract_fusion.ec_ref
  2.3 0.9 copy.4.er_ref
  3.2 2.2 %copy.6 = bf16[96,8,2,256]{3,1,2,0:T(8,128)(2,1)} copy(bf16[96,8,2,256]{3,2,1,0:T(2,128)(2,1)} %bitcast.19) | data formatting | bytes 1572864
  5.4 104.3 %shard_map.37 = f32[768,512]{1,0:T(8,128)} custom-call(bf16[768,512]{1,0:T(8,128)(2,1)} %bitcast.20, f32[4,128,1]{2,1,0:T(8,128)} %copy.4.er_ref, f32[2,512]{1,0:T(2,128)} %broadcast_subtract_fusion.ec_ref), custom_call_target="tpu_custom_call" | custom-call | flops 6442450944 | bytes 2359296 | tf_op jit(solution)/shard_map/pallas_call | solution.py:304
  109.7 3.0 %reshape.28 = f32[768,2,256]{2,1,0:T(2,128)} reshape(f32[768,512]{1,0:T(8,128)} %shard_map.37) | data formatting | bytes 3145728 | tf_op jit(solution)/shard_map/reshape | solution.py:334
  (11 shorter events, 0.1 us)

commit v3 on v2

--- a/solution.py
+++ b/solution.py
@@ -225,6 +225,7 @@
             back(s).start()
 
     number = 0
+    before = []
     for g, group in enumerate(groups):
         if g > 0:
             for h in range(HALVES):
@@ -236,19 +237,24 @@
         for k, s in group:
             named.append((number, k, s))
             number += 1
+        last = g == len(groups) - 1
         for p, k, s in named:
             integrals(p, k, s)
-        last = g == len(groups) - 1
-        for r in range(rounds):
+            for q in before[:1]:
+                finish(*q)
+            before = before[1:]
+        for p, k, s in named:
+            add(p, 0)
+        for q in before:
+            finish(*q)
+        for r in range(1, rounds):
             for p, k, s in named:
                 add(p, r)
                 if r == rounds - 1:
                     amplitudes(p, k, s)
                     if last:
                         finish(p, k, s)
-        if not last:
-            for p, k, s in named:
-                finish(p, k, s)
+        before = [] if last else named
 
     out_ref[...] = dens[0]
     for s in range(1, steps):

time: 113 us -> 105 us (0.929)
  Pallas kernels: 104 us -> 96.1 us
    pallas_call x1, Pallas kernels: 104 us -> 96.1 us  [on_device(): pl.pallas_call(functools.partial(kernel, n_occ, n_virt, n_aux, steps), ou...]
where the time goes in v3:
time: 105 us
  Pallas kernels  96.1 us (92%)
  local copies, waits for them, and re-layouts  7.79 us (7%)
    pallas_call x1, Pallas kernels, on_device(): pl.pallas_call(functools.partial(kernel, n_occ, n_virt, n_aux, steps), ou...  96.1 us
    reshape x1, local copies, waits for them, and re-layouts, on_device(): return density.reshape(factors.shape)  3.05 us
    unnamed x9, local copies, waits for them, and re-layouts  2.35 us

profile of v3, /device:TPU:0, one launch (start us, length us, event | category | flops | bytes accessed | tf_op | source)
XLA Modules:
  0.0 104.6 jit_solution(8003195707345473646)
XLA Ops:
  0.0 0.7 reshape.26
  0.8 0.1 broadcast_bitcast_fusion.3
  0.8 0.1 dynamic-slice
  0.9 0.1 broadcast_bitcast_fusion.1
  1.0 0.7 sub.54
  1.7 0.6 broadcast_subtract_fusion.ec_ref
  2.3 0.9 copy.4.er_ref
  3.2 2.2 %copy.6 = bf16[96,8,2,256]{3,1,2,0:T(8,128)(2,1)} copy(bf16[96,8,2,256]{3,2,1,0:T(2,128)(2,1)} %bitcast.19) | data formatting | bytes 1572864
  5.4 96.1 %shard_map.37 = f32[768,512]{1,0:T(8,128)} custom-call(bf16[768,512]{1,0:T(8,128)(2,1)} %bitcast.20, f32[4,128,1]{2,1,0:T(8,128)} %copy.4.er_ref, f32[2,512]{1,0:T(2,128)} %broadcast_subtract_fusion.ec_ref), custom_call_target="tpu_custom_call" | custom-call | flops 6442450944 | bytes 2359296 | tf_op jit(solution)/shard_map/pallas_call | solution.py:310
  101.5 3.0 %reshape.28 = f32[768,2,256]{2,1,0:T(2,128)} reshape(f32[768,512]{1,0:T(8,128)} %shard_map.37) | data formatting | bytes 3145728 | tf_op jit(solution)/shard_map/reshape | solution.py:340
  (11 shorter events, 0.1 us)

commit v4 on v3

--- a/solution.py
+++ b/solution.py
@@ -202,9 +202,11 @@
         else:
             dens[s] = dens[s] + term
 
-    def back(s):
+    def back(s, h):
+        rows = pl.ds(h * deep, deep)
         return remote(
-            dsend.at[s - 1], drecv.at[s - 1], d_send.at[s - 1], d_recv.at[s - 1], occ=lax.rem(o + s, n_occ)
+            dsend.at[s - 1, rows], drecv.at[s - 1, rows], d_send.at[s - 1, h], d_recv.at[s - 1, h],
+            occ=lax.rem(o + s, n_occ),
         )
 
     groups = [[(0, 0)]]
@@ -219,10 +221,15 @@
     def finish(p, k, s):
         for r in reversed(range(rounds)):
             spread(p, r)
-        contract(p, k, s)
-        if k == n_virt - 1 and s > 0:
-            dsend[s - 1] = dens[s].astype(BF16)
-            back(s).start()
+        if k < n_virt - 1 or s == 0:
+            contract(p, k, s)
+            return
+        for h in range(HALVES):
+            rows = pl.ds(h * deep, deep)
+            left = held[pl.ds(nearest(k, v, n_virt), 1), rows].reshape(deep, block)
+            term = lax.dot_general(left, amps[p], (((1,), (0,)), ((), ())), preferred_element_type=F32)
+            dsend[s - 1, rows] = (dens[s, rows] + term).astype(BF16)
+            back(s, h).start()
 
     number = 0
     before = []
@@ -238,31 +245,54 @@
             named.append((number, k, s))
             number += 1
         last = g == len(groups) - 1
-        for p, k, s in named:
-            integrals(p, k, s)
-            for q in before[:1]:
+        if not last:
+            for p, k, s in named:
+                integrals(p, k, s)
+                for q in before[:1]:
+                    finish(*q)
+                before = before[1:]
+            for p, k, s in named:
+                add(p, 0)
+            for q in before:
                 finish(*q)
-            before = before[1:]
-        for p, k, s in named:
-            add(p, 0)
+            for r in range(1, rounds):
+                for p, k, s in named:
+                    add(p, r)
+                    if r == rounds - 1:
+                        amplitudes(p, k, s)
+            before = named
+            continue
+        for piece in named[:-1]:
+            integrals(*piece)
+        for piece in named[:-1]:
+            add(piece[0], 0)
         for q in before:
             finish(*q)
         for r in range(1, rounds):
-            for p, k, s in named:
-                add(p, r)
-                if r == rounds - 1:
-                    amplitudes(p, k, s)
-                    if last:
-                        finish(p, k, s)
-        before = [] if last else named
-
-    out_ref[...] = dens[0]
+            for piece in named[:-1]:
+                add(piece[0], r)
+        for piece in named[:-1]:
+            amplitudes(*piece)
+        integrals(*named[-1])
+        add(named[-1][0], 0)
+        for piece in named[:-1]:
+            finish(*piece)
+        for r in range(1, rounds):
+            add(named[-1][0], r)
+        amplitudes(*named[-1])
+        finish(*named[-1])
+
+    for h in range(HALVES):
+        rows = pl.ds(h * deep, deep)
+        total = dens[0, rows]
+        for s in range(1, steps):
+            back(s, h).wait_recv()
+            total = total + drecv[s - 1, rows].astype(F32)
+        out_ref[rows] = total
+
     for s in range(1, steps):
-        back(s).wait_recv()
-        out_ref[...] += drecv[s - 1].astype(F32)
-
-    for s in range(1, steps):
-        back(s).wait_send()
+        for h in range(HALVES):
+            back(s, h).wait_send()
         across(s).wait_send()
     for p in range(number):
         for r in range(rounds):
@@ -327,7 +357,7 @@
             pltpu.VMEM((steps - 1, naux, block), BF16),
             dma((2, n_virt, HALVES)), dma((n_virt, HALVES)),
             dma((steps - 1,)), dma((steps - 1,)),
-            dma((steps - 1,)), dma((steps - 1,)),
+            dma((steps - 1, HALVES)), dma((steps - 1, HALVES)),
             dma((pieces, rounds)), dma((pieces, rounds)),
             dma((pieces, rounds)), dma((pieces, rounds)),
             dma((pieces, rounds)), dma((pieces, rounds)),

time: 105 us -> 101 us (0.962)
  Pallas kernels: 96.1 us -> 92.8 us
    pallas_call x1, Pallas kernels: 96.1 us -> 92.8 us  [on_device(): pl.pallas_call(functools.partial(kernel, n_occ, n_virt, n_aux, steps), ou...]
where the time goes in v4:
time: 101 us
  Pallas kernels  92.8 us (92%)
  local copies, waits for them, and re-layouts  7.79 us (8%)
    pallas_call x1, Pallas kernels, on_device(): pl.pallas_call(functools.partial(kernel, n_occ, n_virt, n_aux, steps), ou...  92.8 us
    reshape x1, local copies, waits for them, and re-layouts, on_device(): return density.reshape(factors.shape)  3.05 us
    unnamed x9, local copies, waits for them, and re-layouts  2.35 us

profile of v4, /device:TPU:0, one launch (start us, length us, event | category | flops | bytes accessed | tf_op | source)
XLA Modules:
  0.0 101.2 jit_solution(17325600655119109865)
XLA Ops:
  0.0 0.7 reshape.26
  0.8 0.1 broadcast_bitcast_fusion.3
  0.8 0.1 dynamic-slice
  0.9 0.1 broadcast_bitcast_fusion.1
  1.0 0.7 sub.54
  1.7 0.6 broadcast_subtract_fusion.ec_ref
  2.3 0.9 copy.4.er_ref
  3.2 2.2 %copy.6 = bf16[96,8,2,256]{3,1,2,0:T(8,128)(2,1)} copy(bf16[96,8,2,256]{3,2,1,0:T(2,128)(2,1)} %bitcast.19) | data formatting | bytes 1572864
  5.4 92.8 %shard_map.37 = f32[768,512]{1,0:T(8,128)} custom-call(bf16[768,512]{1,0:T(8,128)(2,1)} %bitcast.20, f32[4,128,1]{2,1,0:T(8,128)} %copy.4.er_ref, f32[2,512]{1,0:T(2,128)} %broadcast_subtract_fusion.ec_ref), custom_call_target="tpu_custom_call" | custom-call | flops 6442450944 | bytes 2359296 | tf_op jit(solution)/shard_map/pallas_call | solution.py:340
  98.2 3.0 %reshape.28 = f32[768,2,256]{2,1,0:T(2,128)} reshape(f32[768,512]{1,0:T(8,128)} %shard_map.37) | data formatting | bytes 3145728 | tf_op jit(solution)/shard_map/reshape | solution.py:370
  (11 shorter events, 0.1 us)
